TPU v7x, 32 devices: a whole 2x2x4 slice. The times are simulated.
32 devices in a mesh: grp: 2 (over x), ex: 8 (over z, y), layer: 2 (over core).
Axes of the slice: x: 2, y: 2, z: 4, core: 2. Of those that a mesh axis runs over, the one named last changes fastest.
Arguments:
- acts: bfloat16 [8192, 8, 256], P(('grp', 'ex'), 'layer'), parts along dimension 0, may hold values from -1.5 to 1.5
- grads: bfloat16 [8192, 8, 256], P(('grp', 'ex'), 'layer'), parts along dimension 0, may hold values from -1.5 to 1.5
- adam_scale: float32 [16, 256], P('grp'), parts along dimension 0, may hold values from 0.2 to 5
- plan: int32 [2, 8], replicated, may hold values from 0 to 7, as said below
- assignment: int32 [8], P('layer'), may hold values from 0 to 7, each once
Outputs:
- scores: float32 [2, 8192, 512], P(None, ('grp', 'ex', 'layer')), parts along dimension 1
There are 2 independent parts, one for each index of `grp`. A program takes and returns all parts, laid end to end along the dimension named above; an argument that names none is the same for every part. Nothing has to cross between parts.
Inputs may be any that keep to these rules, and one draw needn't show every extreme that they name: `plan`: in each round the partner of block b is b XOR m for a nonzero m of that round; rounds have different m.
All inputs are finite; a program needn't handle non-finite values.
Results may differ from a plain program's by a relative error of at most 0.0029.
Values may be sent and summed in bfloat16 or wider, within the bound.
No kernel may reach another device: no remote copies, remote signals or barrier semaphores. Data moves between devices by JAX's collectives and lax.ppermute only.
A program may use at most 64 MiB of HBM per device.

v0:
```python
import jax
import jax.numpy as jnp
from jax import lax
from jax.sharding import PartitionSpec as P


def from_partner(block, axis, stride):
    count = lax.axis_size(axis)
    route = []
    for low in range(count):
        high = low | 1 << stride
        if high != low and high < count:
            route += [(low, high), (high, low)]
    return lax.ppermute(block, axis, route)


def scattered(portion, rows, axis):
    count = rows * lax.axis_size(axis)
    return lax.psum_scatter(portion(jnp.int32(0), count), axis, scatter_dimension=0, tiled=True)


def shards(acts, grads, adam_scale, plan, assignment):
    block_rows = acts.shape[0]
    total_modules = adam_scale.shape[0]
    picker = (assignment[:, None] == jnp.arange(total_modules, dtype=jnp.int32)[None, :]).astype(
        jnp.float32
    )
    scales = jnp.dot(picker, adam_scale, precision=lax.Precision.HIGHEST)
    scaled = (grads.astype(jnp.float32) * scales[None]).astype(jnp.bfloat16)
    position = lax.axis_index("ex")
    bit_count = lax.axis_size("ex").bit_length() - 1
    owned_rows = block_rows // lax.axis_size("layer")
    payload_own = jnp.stack([acts, grads], axis=0)
    round_count = plan.shape[0]
    route_masks = []
    for round_index in range(round_count):
        own_partner = lax.dynamic_index_in_dim(plan[round_index], position, 0, keepdims=False)
        route_masks.append(jnp.bitwise_xor(own_partner, position))

    def partner_payload(route_mask):
        payload = payload_own
        for bit_number in range(bit_count):
            flipped = jnp.bitwise_and(jnp.right_shift(route_mask, bit_number), 1) == 1
            payload = lax.cond(
                flipped,
                lambda held, level=bit_number: from_partner(held, "ex", level),
                lambda held: held,
                payload,
            )
        return payload

    partners = [partner_payload(route_mask) for route_mask in route_masks]

    def tile_term(received):
        act_gram = jnp.einsum("imp,jmp->mij", acts, received[0], preferred_element_type=jnp.float32)
        grad_gram = jnp.einsum(
            "imp,jmp->mij", scaled, received[1], preferred_element_type=jnp.float32
        )
        return jnp.sum(act_gram * grad_gram, axis=0)

    outputs = []
    for received in partners:
        outputs.append(
            scattered(
                lambda first_row, row_count, held=received: tile_term(held), owned_rows, "layer"
            )
        )
    return jnp.stack(outputs, axis=0)


def solution(mesh):
    in_specs = (
        P(("grp", "ex"), "layer", None),
        P(("grp", "ex"), "layer", None),
        P("grp", None),
        P(),
        P("layer"),
    )
    out_specs = P(None, ("grp", "ex", "layer"), None)
    return jax.shard_map(shards, mesh=mesh, in_specs=in_specs, out_specs=out_specs, check_vma=False)
```

profile of v0, /device:TPU:0, one launch (start us, length us, event | category | flops | bytes accessed | tf_op | source)
XLA Modules:
  0.0 233.9 jit_solution(11126460098490977607)
XLA Ops:
  6.5 0.8 fusion.12
  8.6 3.1 %pad_maximum_fusion = bf16[2,512,4,256]{3,2,1,0:T(4,128)(2,1)S(1)} fusion(bf16[1,512,4,256]{3,2,1,0:T(4,128)(2,1)} %bitcast.28, bf16[1,512,4,256]{3,2,1,0:T(4,128)(2,1)} %bitcast.27), kind=kLoop, calls=%fused_computation.4 | loop fusion | flops 1048576 | bytes 4194304 | tf_op jit(solution)/shard_map/stack | solution.py:33
  11.7 48.8 %conditional.6 = (bf16[2,512,4,256]{3,2,1,0:T(4,128)(2,1)}) conditional(s32[]{:T(128)} %convert_element_type.27, bf16[2,512,4,256]{3,2,1,0:T(4,128)(2,1)S(1)} %pad_maximum_fusion, bf16[2,512,4,256]{3,2,1,0:T(4,128)(2,1)S(1)} %pad_maximum_fusion), branch_computations={%region_0.1_spmd, %region_1.2_spmd} | conditional | bytes 8388656 | solution.py:44
  11.7 3.0 %collective-permute-start = (bf16[2,512,4,256]{3,2,1,0:T(4,128)(2,1)S(1)}, bf16[2,512,4,256]{3,2,1,0:T(4,128)(2,1)}, u32[]{:S(2)}, u32[]{:S(2)}) collective-permute-start(bf16[2,512,4,256]{3,2,1,0:T(4,128)(2,1)S(1)} %param.1), channel_id=1, source_target_pairs={{0,2},{2,0},{4,6},{6,4},{8,10},{10,8},{12,14},{14,12},{1,3},{3,1},... | collective-permute-start | bytes 6291464 | tf_op jit(solution)/shard_map/cond/branch_1_fun/ppermute | solution.py:14
  14.7 45.7 %collective-permute-done = bf16[2,512,4,256]{3,2,1,0:T(4,128)(2,1)} collective-permute-done((bf16[2,512,4,256]{3,2,1,0:T(4,128)(2,1)S(1)}, bf16[2,512,4,256]{3,2,1,0:T(4,128)(2,1)}, u32[]{:S(2)}, u32[]{:S(2)}) %collective-permute-start) | collective-permute-done | bytes 2097184 | tf_op jit(solution)/shard_map/cond/branch_1_fun/ppermute | solution.py:14
  60.5 2.4 %fusion.10 = (bf16[1,512,4,256]{3,2,1,0:T(4,128)(2,1)S(1)}, bf16[1,512,4,256]{3,2,1,0:T(4,128)(2,1)S(1)}) fusion(bf16[2,512,4,256]{3,2,1,0:T(4,128)(2,1)} %get-tuple-element.45), kind=kLoop, calls=%fused_computation.22 | loop fusion | bytes 4194304 | tf_op jit(solution)/shard_map/slice | solution.py:57
  62.9 0.7 fusion.3
  64.5 1.8 fusion.1
  67.1 1.3 conditional.9
  67.1 1.3 copy.49
  68.4 48.4 %conditional.10 = (bf16[2,512,4,256]{3,2,1,0:T(4,128)(2,1)}) conditional(s32[]{:T(128)} %convert_element_type.31, bf16[2,512,4,256]{3,2,1,0:T(4,128)(2,1)} %get-tuple-element.46, bf16[2,512,4,256]{3,2,1,0:T(4,128)(2,1)} %get-tuple-element.46), branch_computations={%region_10.11_spmd, %region_11.12_spmd} | conditional | bytes 12582960 | solution.py:44
  68.4 1.8 collective-permute-start.4
  70.2 45.2 %collective-permute-done.4 = bf16[2,512,4,256]{3,2,1,0:T(4,128)(2,1)S(1)} collective-permute-done((bf16[2,512,4,256]{3,2,1,0:T(4,128)(2,1)}, bf16[2,512,4,256]{3,2,1,0:T(4,128)(2,1)S(1)}, u32[]{:S(2)}, u32[]{:S(2)}) %collective-permute-start.4) | collective-permute-done | bytes 2097184 | tf_op jit(solution)/shard_map/cond/branch_1_fun/ppermute | solution.py:14
  115.4 1.3 copy.52
  116.8 93.3 %conditional.11 = (bf16[2,512,4,256]{3,2,1,0:T(4,128)(2,1)}) conditional(s32[]{:T(128)} %convert_element_type.30, bf16[2,512,4,256]{3,2,1,0:T(4,128)(2,1)} %get-tuple-element.47, bf16[2,512,4,256]{3,2,1,0:T(4,128)(2,1)} %get-tuple-element.47), branch_computations={%region_12.13_spmd, %region_13.14_spmd} | conditional | bytes 12582960 | solution.py:44
  116.8 2.5 %collective-permute-start.5 = (bf16[2,512,4,256]{3,2,1,0:T(4,128)(2,1)}, bf16[2,512,4,256]{3,2,1,0:T(4,128)(2,1)S(1)}, u32[]{:S(2)}, u32[]{:S(2)}) collective-permute-start(bf16[2,512,4,256]{3,2,1,0:T(4,128)(2,1)} %param.11), channel_id=1, source_target_pairs={{0,8},{8,0},{2,10},{10,2},{4,12},{12,4},{6,14},{14,6},{1,9},{9,1},... | collective-permute-start | bytes 6291464 | tf_op jit(solution)/shard_map/cond/branch_1_fun/ppermute | solution.py:14
  119.3 89.5 %collective-permute-done.5 = bf16[2,512,4,256]{3,2,1,0:T(4,128)(2,1)S(1)} collective-permute-done((bf16[2,512,4,256]{3,2,1,0:T(4,128)(2,1)}, bf16[2,512,4,256]{3,2,1,0:T(4,128)(2,1)S(1)}, u32[]{:S(2)}, u32[]{:S(2)}) %collective-permute-start.5) | collective-permute-done | bytes 2097184 | tf_op jit(solution)/shard_map/cond/branch_1_fun/ppermute | solution.py:14
  208.7 1.3 copy.54
  210.1 2.3 %fusion.11 = (bf16[1,512,4,256]{3,2,1,0:T(4,128)(2,1)S(1)}, bf16[1,512,4,256]{3,2,1,0:T(4,128)(2,1)S(1)}) fusion(bf16[2,512,4,256]{3,2,1,0:T(4,128)(2,1)} %get-tuple-element.48), kind=kLoop, calls=%fused_computation.23 | loop fusion | bytes 4194304 | tf_op jit(solution)/shard_map/slice | solution.py:57
  212.4 0.8 fusion.2
  213.2 1.8 fusion
  215.1 9.4 %reduce-scatter.5.cloned.1.call-done = f32[256,512]{0,1:T(8,128)} async-done(((f32[512,512]{0,1:T(8,128)}), f32[256,512]{0,1:T(8,128)}) %reduce-scatter.5.cloned.1.call-update) | async-done | bytes 524304 | tf_op jit(solution)/shard_map/reduce_scatter | solution.py:19
  224.5 1.3 pad_maximum_fusion.1
  225.7 1.3 copy.26
  (20 shorter events, 1.6 us)
Async XLA Ops:
  6.5 57.1 %copy-start = (f32[8,256]{1,0:T(8,128)S(1)}, f32[8,256]{1,0:T(8,128)}, u32[]{:S(2)}) copy-start(f32[8,256]{1,0:T(8,128)} %param.19) | copy-start | bytes 24580
  6.5 208.5 %reduce-scatter.3.cloned.1.call-start = ((), (), s32[]{:S(2)}) async-start(), calls=%async_computation.2 | async-start | bytes 1572864 | tf_op jit(solution)/shard_map/reduce_scatter | solution.py:19
  11.7 48.8 %collective-permute-start = (bf16[2,512,4,256]{3,2,1,0:T(4,128)(2,1)S(1)}, bf16[2,512,4,256]{3,2,1,0:T(4,128)(2,1)}, u32[]{:S(2)}, u32[]{:S(2)}) collective-permute-start(bf16[2,512,4,256]{3,2,1,0:T(4,128)(2,1)S(1)} %param.1), channel_id=1, source_target_pairs={{0,2},{2,0},{4,6},{6,4},{8,10},{10,8},{12,14},{14,12},{1,3},{3,1},... | collective-permute-start | bytes 6291464 | tf_op jit(solution)/shard_map/cond/branch_1_fun/ppermute | solution.py:14
  60.5 2.4 %copy-start.1 = (bf16[512,4,256]{2,1,0:T(4,128)(2,1)S(1)}, bf16[512,4,256]{2,1,0:T(4,128)(2,1)}, u32[]{:S(2)}) copy-start(bf16[512,4,256]{2,1,0:T(4,128)(2,1)} %param.17) | copy-start | bytes 3145732
  62.8 0.8 copy-start.4
  62.9 1.2 copy-start.3
  66.4 158.1 %reduce-scatter.5.cloned.1.call-start = ((), (), s32[]{:S(2)}) async-start(), calls=%async_computation.3 | async-start | bytes 1572864 | tf_op jit(solution)/shard_map/reduce_scatter | solution.py:19
  68.4 47.0 %collective-permute-start.4 = (bf16[2,512,4,256]{3,2,1,0:T(4,128)(2,1)}, bf16[2,512,4,256]{3,2,1,0:T(4,128)(2,1)S(1)}, u32[]{:S(2)}, u32[]{:S(2)}) collective-permute-start(bf16[2,512,4,256]{3,2,1,0:T(4,128)(2,1)} %param.9), channel_id=1, source_target_pairs={{0,4},{4,0},{2,6},{6,2},{8,12},{12,8},{10,14},{14,10},{1,5},{5,1},... | collective-permute-start | bytes 6291464 | tf_op jit(solution)/shard_map/cond/branch_1_fun/ppermute | solution.py:14
  116.8 91.9 %collective-permute-start.5 = (bf16[2,512,4,256]{3,2,1,0:T(4,128)(2,1)}, bf16[2,512,4,256]{3,2,1,0:T(4,128)(2,1)S(1)}, u32[]{:S(2)}, u32[]{:S(2)}) collective-permute-start(bf16[2,512,4,256]{3,2,1,0:T(4,128)(2,1)} %param.11), channel_id=1, source_target_pairs={{0,8},{8,0},{2,10},{10,2},{4,12},{12,4},{6,14},{14,6},{1,9},{9,1},... | collective-permute-start | bytes 6291464 | tf_op jit(solution)/shard_map/cond/branch_1_fun/ppermute | solution.py:14
  210.1 2.4 %copy-start.2 = (bf16[512,4,256]{2,1,0:T(4,128)(2,1)S(1)}, bf16[512,4,256]{2,1,0:T(4,128)(2,1)}, u32[]{:S(2)}) copy-start(bf16[512,4,256]{2,1,0:T(4,128)(2,1)} %param.17) | copy-start | bytes 3145732
Sparse Core Ops, SparseCore 0:
  66.5 10.0 reduce-scatter.2
  215.2 9.2 reduce-scatter.4
where the time goes:
time: 234 us
  waiting for transfers between devices  190 us (81%)
  between operations  14.8 us (6%)
  local copies, waits for them, and re-layouts  11.7 us (5%)
  starting transfers between devices  7.36 us (3%)
  matrix products  5.36 us (2%)
  other arithmetic  4.79 us (2%)
    ppermute x3, waiting for transfers between devices, from_partner(): return lax.ppermute(block, axis, route)  180 us
    reduce_scatter x2, waiting for transfers between devices, scattered(): lax.psum_scatter(portion(jnp.int32(0), count), axis, scatter_dimension=0,...  9.43 us
    ppermute x3, starting transfers between devices, from_partner(): return lax.ppermute(block, axis, route)  7.32 us
    slice x2, local copies, waits for them, and re-layouts, tile_term(): received[1]  4.7 us
  transfers between devices with their start and end apart: 5, of which 4 were waited for; matrix products, arithmetic and copies ran while one was open for 4% of the time, Pallas kernels for 0%

commit v1 on v0

v1 whole, which is shorter than its diff:
```python
import jax
import jax.numpy as jnp
from jax import lax
from jax.sharding import PartitionSpec as P

MOST_BLOCKS = 8


def parity(number):
    return bin(number).count("1") & 1


def module_major(rows):
    return jnp.transpose(rows, (1, 0, 2))


def gram_sum(own_acts, own_scaled, partner):
    act_gram = jnp.einsum("mip,mjp->mij", own_acts, partner[0], preferred_element_type=jnp.float32)
    grad_gram = jnp.einsum("mip,mjp->mij", own_scaled, partner[1], preferred_element_type=jnp.float32)
    return jnp.sum(act_gram * grad_gram, axis=0)


def busiest(low, high, vector, count):
    load = {}
    for block in range(count):
        end = block ^ (low if parity(block & vector) else high)
        at, to = block >> 1, end >> 1
        step = 1 if to > at else -1
        while at != to:
            load[at, block & 1, step] = load.get((at, block & 1, step), 0) + 1
            at += step
        if (block ^ end) & 1:
            load[to, block & 1, 0] = load.get((to, block & 1, 0), 0) + 1
    return max(load.values())


def colouring(low, high, count):
    found = [vector for vector in range(1, count) if parity(vector & low) and parity(vector & high)]
    return min(found, key=lambda vector: busiest(low, high, vector, count))


def routes(low, high, count):
    vector = colouring(low, high, count)
    feed, reply = [], []
    for block in range(count):
        own, other = (high, low) if parity(block & vector) else (low, high)
        feed.append((block, block ^ other))
        reply.append((block, block ^ own))
    return feed, reply


def paired_rounds(own_acts, own_grads, own_scaled, plan):
    count = lax.axis_size("ex")
    core = lax.axis_index("layer")
    half = own_acts.shape[1] // 2
    first, second = plan[0, 0], plan[1, 0]
    low, high = jnp.minimum(first, second), jnp.maximum(first, second)
    pairs = [(a, b) for b in range(2, count) for a in range(1, b)]
    index = (high - 1) * (high - 2) // 2 + low - 1
    plans = [routes(a, b, count) for a, b in pairs]
    vectors = jnp.array([colouring(a, b, count) for a, b in pairs], jnp.int32)
    received = lax.switch(
        index,
        [lambda held, feed=feed: lax.ppermute(held, "ex", feed) for feed, _ in plans],
        jnp.stack([own_acts, own_grads]),
    )
    tile = gram_sum(own_acts, own_scaled, received)

    kept = lax.dynamic_slice_in_dim(tile, core * half, half, 0)
    passed = lax.dynamic_slice_in_dim(tile, (1 - core) * half, half, 0)
    corner = lax.dynamic_slice_in_dim(kept, (1 - core) * half, half, 1)
    swap = [(0, 1), (1, 0)]
    across = lax.ppermute(jnp.concatenate([passed, corner], axis=1), "layer", swap)
    own = kept + across[:, : 2 * half]
    same = lax.dynamic_slice_in_dim(own, core * half, half, 1)
    cross = lax.dynamic_slice_in_dim(passed, core * half, half, 1) + across[:, 2 * half :]
    turned = jnp.where(
        core == 0, jnp.concatenate([same, cross], axis=0), jnp.concatenate([cross, same], axis=0)
    ).T.astype(jnp.bfloat16)
    other = lax.switch(
        index,
        [lambda held, reply=reply: lax.ppermute(held, "ex", reply) for _, reply in plans],
        turned,
    ).astype(jnp.float32)

    marked = jnp.bitwise_and(lax.axis_index("ex"), vectors[index])
    colour = lax.population_count(marked) & 1
    own_first = (colour == 0) == (first < second)
    return jnp.stack([jnp.where(own_first, own, other), jnp.where(own_first, other, own)])


def direct_rounds(own_acts, own_grads, own_scaled, plan):
    count = lax.axis_size("ex")
    payload = jnp.stack([own_acts, own_grads])
    outputs = []
    for round_index in range(plan.shape[0]):
        branches = [
            lambda held, mask=mask: lax.ppermute(
                held, "ex", [(block, block ^ mask) for block in range(count)]
            )
            for mask in range(1, count)
        ]
        received = lax.switch(plan[round_index, 0] - 1, branches, payload)
        tile = gram_sum(own_acts, own_scaled, received)
        outputs.append(lax.psum_scatter(tile, "layer", scatter_dimension=0, tiled=True))
    return jnp.stack(outputs)


def shards(acts, grads, adam_scale, plan, assignment):
    total_modules = adam_scale.shape[0]
    count = lax.axis_size("ex")
    picker = (assignment[:, None] == jnp.arange(total_modules, dtype=jnp.int32)[None, :]).astype(
        jnp.float32
    )
    scales = jnp.dot(picker, adam_scale, precision=lax.Precision.HIGHEST)
    own_acts, own_grads = module_major(acts), module_major(grads)
    own_scaled = (own_grads.astype(jnp.float32) * scales[:, None, :]).astype(jnp.bfloat16)
    if count > MOST_BLOCKS:
        return direct_rounds(own_acts, own_grads, own_scaled, plan)
    return paired_rounds(own_acts, own_grads, own_scaled, plan)


def solution(mesh):
    in_specs = (
        P(("grp", "ex"), "layer", None),
        P(("grp", "ex"), "layer", None),
        P("grp", None),
        P(),
        P("layer"),
    )
    out_specs = P(None, ("grp", "ex", "layer"), None)
    return jax.shard_map(shards, mesh=mesh, in_specs=in_specs, out_specs=out_specs, check_vma=False)
```

time: 234 us -> 79.7 us (0.34)
  waiting for transfers between devices: 190 us -> 52.9 us
  between operations: 14.8 us -> 4.89 us
  local copies, waits for them, and re-layouts: 11.7 us -> 6.38 us
  other arithmetic: 4.79 us -> 0.76 us
    ppermute x3, waiting for transfers between devices: 180 us -> 52.9 us  [the longest x1 44.9 us: paired_rounds(): lax.ppermute(held, 'ex', feed)]
    reduce_scatter x2 -> x0, waiting for transfers between devices: 9.43 us -> none  [scattered(): lax.psum_scatter(portion(jnp.int32(0), count), axis, scatter_dimension=0,...]
    slice x3 -> x1, local copies, waits for them, and re-layouts: 5.46 us -> 1.35 us  [paired_rounds(): first, second = (plan[0, 0], plan[1, 0])]
    another operation x2 -> x3, other arithmetic: 4.38 us -> 0.34 us  [the longest x1 0.19 us: paired_rounds(): jnp.stack([own_acts, own_grads])]
    cond x3 -> x0, local copies, waits for them, and re-layouts: 4.01 us -> none
    another operation x1 -> x3, local copies, waits for them, and re-layouts: 1.31 us -> 4.21 us  [the longest x1 1.82 us: paired_rounds(): jnp.stack([own_acts, own_grads])]
    dot_general x4 -> x2, matrix products: 5.17 us -> 7.49 us  [the longest x1 4.01 us: gram_sum(): jnp.einsum('mip,mjp->mij', own_acts, partner[0], preferred_element_type=j...]
  transfers between devices with their start and end apart: 5 -> 3, of which waited for: 4 -> 2; matrix products, arithmetic and copies ran while one was open for 4% -> 1% of each run, Pallas kernels for 0% -> 0%
where the time goes in v1:
time: 79.7 us; the launch traced here: 79.4 us
  waiting for transfers between devices  52.9 us (66%)
  matrix products  7.67 us (10%)
  starting transfers between devices  6.69 us (8%)
  local copies, waits for them, and re-layouts  6.38 us (8%)
  between operations  4.89 us (6%)
    ppermute x1, waiting for transfers between devices, paired_rounds(): lax.ppermute(held, 'ex', feed)  44.9 us
    ppermute x1, waiting for transfers between devices, paired_rounds(): lax.ppermute(held, 'ex', reply)  8.04 us
    ppermute x1, starting transfers between devices, paired_rounds(): lax.ppermute(held, 'ex', feed)  4.03 us
    dot_general x1, matrix products, gram_sum(): jnp.einsum('mip,mjp->mij', own_acts, partner[0], preferred_element_type=j...  4.01 us
    dot_general x1, matrix products, gram_sum(): jnp.einsum('mip,mjp->mij', own_scaled, partner[1], preferred_element_type...  3.48 us
    ppermute x1, starting transfers between devices, paired_rounds(): lax.ppermute(held, 'ex', reply)  2.58 us
    another operation x1, local copies, waits for them, and re-layouts, paired_rounds(): jnp.stack([own_acts, own_grads])  1.82 us
  transfers between devices with their start and end apart: 3, of which 2 were waited for; matrix products, arithmetic and copies ran while one was open for 1% of the time, Pallas kernels for 0%

profile of v1, /device:TPU:0, one launch (start us, length us, event | category | flops | bytes accessed | tf_op | source)
XLA Modules:
  0.0 79.4 jit_solution(13610017191527181036)
XLA Ops:
  0.0 1.3 %fusion.13 = (s32[1,1]{1,0:T(1,128)}, s32[1,1]{1,0:T(1,128)}) fusion(s32[2,8]{1,0:T(2,128)} %param.51), kind=kLoop, calls=%fused_computation.30 | loop fusion | bytes 16 | tf_op jit(solution)/shard_map/slice | solution.py:56
  4.1 1.8 %copy_bitcast_fusion = (bf16[1,4,512,256]{3,2,1,0:T(8,128)(2,1)S(1)}, bf16[1,4,512,256]{3,2,1,0:T(8,128)(2,1)S(1)}) fusion(bf16[512,4,256]{2,1,0:T(4,128)(2,1)} %param.49, bf16[512,4,256]{2,1,0:T(4,128)(2,1)} %param.48), kind=kLoop, calls=%fused_computation.11 | loop fusion | bytes 4194304 | tf_op jit(solution)/shard_map/stack | solution.py:65
  5.9 0.2 pad_maximum_fusion
  6.1 48.9 %conditional.5 = (bf16[2,4,512,256]{3,2,1,0:T(8,128)(2,1)}) conditional(s32[]{:T(128)} %clamp.12, bf16[2,4,512,256]{3,2,1,0:T(8,128)(2,1)S(1)} %pad_maximum_fusion, bf16[2,4,512,256]{3,2,1,0:T(8,128)(2,1)S(1)} %pad_maximum_fusion, bf16[2,4,512,256]{3,2,1,0:T(8,128)(2,1)S(1)} %pad_maximum_fusion, ...), branch_computations={%region_0.1_spmd, %region_1.2_spmd, %region_2.3_spmd, %region_3.4_... | conditional | bytes 8388656 | solution.py:62
  6.1 4.0 %collective-permute-start.2 = (bf16[2,4,512,256]{3,2,1,0:T(8,128)(2,1)S(1)}, bf16[2,4,512,256]{3,2,1,0:T(8,128)(2,1)}, u32[]{:S(2)}, u32[]{:S(2)}) collective-permute-start(bf16[2,4,512,256]{3,2,1,0:T(8,128)(2,1)S(1)} %param.2), channel_id=1, source_target_pairs={{0,6},{2,4},{4,0},{6,2},{8,14},{10,12},{12,8},{14,10},{1,7},{3,5},... | collective-permute-start | bytes 6291464 | tf_op jit(solution)/shard_map/cond/branch_2_fun/ppermute | solution.py:64
  10.2 44.9 %collective-permute-done.2 = bf16[2,4,512,256]{3,2,1,0:T(8,128)(2,1)} collective-permute-done((bf16[2,4,512,256]{3,2,1,0:T(8,128)(2,1)S(1)}, bf16[2,4,512,256]{3,2,1,0:T(8,128)(2,1)}, u32[]{:S(2)}, u32[]{:S(2)}) %collective-permute-start.2) | collective-permute-done | bytes 2097184 | tf_op jit(solution)/shard_map/cond/branch_2_fun/ppermute | solution.py:64
  55.1 4.0 %fusion.1 = f32[4,512,512]{2,1,0:T(8,128)} fusion(bf16[2,4,512,256]{3,2,1,0:T(8,128)(2,1)} %get-tuple-element.103, bf16[512,4,256]{2,1,0:T(4,128)(2,1)S(1)} %copy-done.2), kind=kOutput, calls=%fused_computation.6 | convolution fusion | flops 536870912 | bytes 6291456 | tf_op jit(solution)/shard_map/mip,mjp->mij/dot_general | solution.py:18
  59.1 0.2 fusion.11
  59.3 3.5 %fusion = f32[512,512]{0,1:T(8,128)S(1)} fusion(f32[4,512,512]{2,1,0:T(8,128)} %fusion.1, bf16[2,4,512,256]{3,2,1,0:T(8,128)(2,1)} %get-tuple-element.103, f32[4,256]{1,0:T(4,128)S(1)} %fusion.11, bf16[512,4,256]{2,1,0:T(4,128)(2,1)S(1)} %copy-done.1), kind=kOutput, calls=%fused_computation.1 | convolution fusion | flops 540278784 | bytes 7344128 | tf_op jit(solution)/shard_map/mip,mjp->mij/dot_general | solution.py:19
  62.7 0.0 copy-start.4
  62.8 0.1 dynamic_slice.21
  63.0 0.1 pad_maximum_fusion.2
  63.0 0.1 collective-permute-start.42
  64.5 0.6 dynamic_slice.18
  65.7 0.1 slice_add_fusion
  65.9 0.2 slice_add_fusion.1
  66.0 0.1 fusion.10
  66.2 10.6 %conditional.6 = (bf16[256,512]{1,0:T(8,128)(2,1)}) conditional(s32[]{:T(128)} %clamp.12, bf16[256,512]{1,0:T(8,128)(2,1)S(1)} %fusion.10, bf16[256,512]{1,0:T(8,128)(2,1)S(1)} %fusion.10, bf16[256,512]{1,0:T(8,128)(2,1)S(1)} %fusion.10, bf16[256,512]{1,0:T(8,128)(2,1)S(1)} %fusion.10, ...), branch_computations={%region_22.23_spmd, %region_23.24_spmd, %region_24.25_spmd, %regio... | conditional | bytes 1048624
  66.2 2.6 %collective-permute-start.23 = (bf16[256,512]{1,0:T(8,128)(2,1)S(1)}, bf16[256,512]{1,0:T(8,128)(2,1)}, u32[]{:S(2)}, u32[]{:S(2)}) collective-permute-start(bf16[256,512]{1,0:T(8,128)(2,1)S(1)} %param.23), channel_id=1, source_target_pairs={{0,4},{2,6},{4,2},{6,0},{8,12},{10,14},{12,10},{14,8},{1,5},{3,7},... | collective-permute-start | bytes 786440 | tf_op jit(solution)/shard_map/cond/branch_2_fun/ppermute | solution.py:82
  68.8 8.0 %collective-permute-done.23 = bf16[256,512]{1,0:T(8,128)(2,1)} collective-permute-done((bf16[256,512]{1,0:T(8,128)(2,1)S(1)}, bf16[256,512]{1,0:T(8,128)(2,1)}, u32[]{:S(2)}, u32[]{:S(2)}) %collective-permute-start.23) | collective-permute-done | bytes 262176 | tf_op jit(solution)/shard_map/cond/branch_2_fun/ppermute | solution.py:82
  76.8 1.1 %copy.34 = bf16[256,512]{0,1:T(8,128)(2,1)S(1)} copy(bf16[256,512]{1,0:T(8,128)(2,1)} %get-tuple-element.104) | data formatting | bytes 524288 | tf_op jit(solution)/shard_map/conditional.1
  77.9 0.1 fusion.7
  78.0 0.1 pad_maximum_fusion.1
  78.1 1.3 %copy.35 = f32[2,256,512]{2,1,0:T(8,128)} copy(f32[2,256,512]{1,2,0:T(8,128)S(1)} %pad_maximum_fusion.1) | data formatting | bytes 2097152 | tf_op jit(solution)/shard_map/stack | solution.py:89
  (12 shorter events, 0.1 us)
Async XLA Ops:
  0.0 59.1 %copy-start = (f32[8,256]{1,0:T(8,128)S(1)}, f32[8,256]{1,0:T(8,128)}, u32[]{:S(2)}) copy-start(f32[8,256]{1,0:T(8,128)} %param.50) | copy-start | bytes 24580
  5.9 49.2 %copy-start.2 = (bf16[512,4,256]{2,1,0:T(4,128)(2,1)S(1)}, bf16[512,4,256]{2,1,0:T(4,128)(2,1)}, u32[]{:S(2)}) copy-start(bf16[512,4,256]{2,1,0:T(4,128)(2,1)} %param.48) | copy-start | bytes 3145732
  6.1 48.9 %collective-permute-start.2 = (bf16[2,4,512,256]{3,2,1,0:T(8,128)(2,1)S(1)}, bf16[2,4,512,256]{3,2,1,0:T(8,128)(2,1)}, u32[]{:S(2)}, u32[]{:S(2)}) collective-permute-start(bf16[2,4,512,256]{3,2,1,0:T(8,128)(2,1)S(1)} %param.2), channel_id=1, source_target_pairs={{0,6},{2,4},{4,0},{6,2},{8,14},{10,12},{12,8},{14,10},{1,7},{3,5},... | collective-permute-start | bytes 6291464 | tf_op jit(solution)/shard_map/cond/branch_2_fun/ppermute | solution.py:64
  55.1 4.0 %copy-start.3 = (s32[4]{0:T(128)S(1)}, s32[4]{0:T(128)}, u32[]{:S(2)}) copy-start(s32[4]{0:T(128)} %param.52) | copy-start | bytes 52
  55.1 4.2 %copy-start.1 = (bf16[512,4,256]{2,1,0:T(4,128)(2,1)S(1)}, bf16[512,4,256]{2,1,0:T(4,128)(2,1)}, u32[]{:S(2)}) copy-start(bf16[512,4,256]{2,1,0:T(4,128)(2,1)} %param.49) | copy-start | bytes 3145732
  62.7 1.7 %copy-start.4 = (s32[21]{0:T(128)S(1)}, s32[21]{0:T(128)}, u32[]{:S(2)}) copy-start(s32[21]{0:T(128)} %constant.63.clone) | copy-start | bytes 256
  63.0 2.7 %collective-permute-start.42 = (f32[256,768]{0,1:T(8,128)S(1)}, f32[256,768]{0,1:T(8,128)S(1)}, u32[]{:S(2)}, u32[]{:S(2)}) collective-permute-start(f32[256,768]{0,1:T(8,128)S(1)} %pad_maximum_fusion.2), channel_id=1, source_target_pairs={{0,1},{1,0},{2,3},{3,2},{4,5},{5,4},{6,7},{7,6},{8,9},{9,8},{10,11... | collective-permute-start | bytes 2359304 | tf_op jit(solution)/shard_map/ppermute | solution.py:73
  66.2 10.6 %collective-permute-start.23 = (bf16[256,512]{1,0:T(8,128)(2,1)S(1)}, bf16[256,512]{1,0:T(8,128)(2,1)}, u32[]{:S(2)}, u32[]{:S(2)}) collective-permute-start(bf16[256,512]{1,0:T(8,128)(2,1)S(1)} %param.23), channel_id=1, source_target_pairs={{0,4},{2,6},{4,2},{6,0},{8,12},{10,14},{12,10},{14,8},{1,5},{3,7},... | collective-permute-start | bytes 786440 | tf_op jit(solution)/shard_map/cond/branch_2_fun/ppermute | solution.py:82
